TPU v7x, 32 devices: a whole 2x2x4 slice. The times are simulated.
32 devices in a mesh: seq: 8 (over z, x), head: 4 (over y, core).
Axes of the slice: x: 2, y: 2, z: 4, core: 2. Of those that a mesh axis runs over, the one named last changes fastest.
Arguments:
- query: bfloat16 [2048, 1024], P('seq', 'head'), may hold values from -20 to 20
- key_states: bfloat16 [2048, 1024], P('seq', 'head'), may hold values from -20 to 20
- values: bfloat16 [2048, 1024], P('seq', 'head'), may hold values from -6 to 6
- grad_out: bfloat16 [2048, 1024], P('seq', 'head'), may hold values from -6 to 6
- rand_blocks: int32 [32, 2], replicated, may hold values from 0 to 31, as said below
- global_blocks: int32 [2], replicated, may hold values from 0 to 31, as said below
Outputs:
- out: bfloat16 [2048, 1024], P('seq', 'head')
- dq: bfloat16 [2048, 1024], P('seq', 'head')
- dk: bfloat16 [2048, 1024], P('seq', 'head')
- dv: bfloat16 [2048, 1024], P('seq', 'head')
Inputs may be any that keep to these rules, and one draw needn't show every extreme that they name: `rand_blocks`: take the query blocks of one index of seq (aligned runs of 4 rows). Among their 8 entries at most 2 lie in the blocks of any one index o (blocks o*4 to o*4 + 3), and for every run some index receives exactly 2 of them. `global_blocks`: 2 different block numbers; the last of them is the sequence's last block.
All inputs are finite; a program needn't handle non-finite values.
Results may differ from a plain program's by a relative error of at most 0.04.
Values may be sent and summed in bfloat16 or wider, within the bound.
A program may use at most 128 MiB of HBM per device.

v0:
```python
import math
import jax
import jax.numpy as jnp
from jax import lax
from jax.sharding import PartitionSpec as P

HEAD_SIZE = 128
BLOCK_TOKENS = 64


def extended_2(block, sides, width):
    for axis, dim in sides:
        count = lax.axis_size(axis)
        forward = [(i, i + 1) for i in range(count - 1)]
        forward.append((count - 1, 0))
        backward = [(target, source) for source, target in forward]
        low = lax.ppermute(
            lax.slice_in_dim(block, block.shape[dim] - width, None, axis=dim), axis, forward
        )
        high = lax.ppermute(lax.slice_in_dim(block, 0, width, axis=dim), axis, backward)
        block = jnp.concatenate([low, block, high], axis=dim)
    return block


def shards(query, key_states, values, grad_out, rand_blocks, global_blocks):
    tokens, feature_width = query.shape
    head_count = feature_width // HEAD_SIZE
    nshard = lax.axis_size("seq")
    myself = lax.axis_index("seq")
    block_count = tokens // BLOCK_TOKENS
    nrand = rand_blocks.shape[1]
    nglob = global_blocks.shape[0]
    nfixed = 3 + nglob
    needed = block_count * nrand
    slots = max(2, (needed + nshard - 1) // nshard)
    double_width = 2 * feature_width
    score_scale = 1.0 / math.sqrt(HEAD_SIZE)
    paired = jnp.concatenate([key_states, values], axis=1)
    paired_blocks = paired.reshape(block_count, BLOCK_TOKENS, double_width)
    extended = extended_2(paired, (("seq", 0),), BLOCK_TOKENS)
    owners_glob = global_blocks // block_count
    local_glob = global_blocks % block_count
    pieces = []
    for glob_index in range(nglob):
        piece = lax.dynamic_slice_in_dim(
            paired, local_glob[glob_index] * BLOCK_TOKENS, BLOCK_TOKENS, 0
        )
        pieces.append(jnp.where(owners_glob[glob_index] == myself, piece.astype(jnp.float32), 0.0))
    global_rows = lax.psum(jnp.concatenate(pieces, axis=0), "seq").astype(jnp.bfloat16)
    table = rand_blocks.reshape(nshard, needed)
    owner_table = table // block_count
    local_table = table % block_count
    position = jnp.arange(needed)
    earlier_same = (owner_table[:, :, None] == owner_table[:, None, :]) & (
        position[None, None, :] < position[None, :, None]
    )
    rank_table = jnp.sum(earlier_same.astype(jnp.int32), axis=2)
    slot_range = jnp.arange(slots)
    matched = (owner_table[:, :, None] == myself) & (
        rank_table[:, :, None] == slot_range[None, None, :]
    )
    valid = jnp.any(matched, axis=1)
    send_local = jnp.sum(jnp.where(matched, local_table[:, :, None], 0), axis=1)
    outgoing = jnp.where(
        valid[:, :, None, None], paired_blocks[send_local], jnp.zeros((), jnp.bfloat16)
    )
    incoming = lax.all_to_all(outgoing, "seq", split_axis=0, concat_axis=0, tiled=True)
    my_owner = lax.dynamic_index_in_dim(owner_table, myself, 0, keepdims=False)
    my_rank = lax.dynamic_index_in_dim(rank_table, myself, 0, keepdims=False)
    flat_slot = my_owner * slots + my_rank
    fetched = incoming.reshape(nshard * slots, BLOCK_TOKENS, double_width)[flat_slot].reshape(
        block_count, nrand, BLOCK_TOKENS, double_width
    )
    ext_blocks = extended.reshape(block_count + 2, BLOCK_TOKENS, double_width)
    window_blocks = jnp.stack([ext_blocks[:-2], ext_blocks[1:-1], ext_blocks[2:]], axis=1)
    glob_wide = jnp.broadcast_to(
        global_rows.reshape(1, nglob, BLOCK_TOKENS, double_width),
        (block_count, nglob, BLOCK_TOKENS, double_width),
    )
    gathered = jnp.concatenate([window_blocks, glob_wide, fetched], axis=1)
    key_count = gathered.shape[1]
    key_matrix = gathered[..., :feature_width].reshape(
        block_count, key_count * BLOCK_TOKENS, head_count, HEAD_SIZE
    )
    value_matrix = gathered[..., feature_width:].reshape(
        block_count, key_count * BLOCK_TOKENS, head_count, HEAD_SIZE
    )
    query_matrix = query.reshape(block_count, BLOCK_TOKENS, head_count, HEAD_SIZE)
    logit_scores = (
        jnp.einsum("bqhd,bkhd->bhqk", query_matrix, key_matrix, preferred_element_type=jnp.float32)
        * score_scale
    )
    top = jnp.max(logit_scores, axis=-1, keepdims=True)
    lse = top + jnp.log(jnp.sum(jnp.exp(logit_scores - top), axis=-1, keepdims=True))
    probs = jnp.exp(logit_scores - lse)
    softmax_weights = probs.astype(jnp.bfloat16)
    attended_output = jnp.einsum(
        "bhqk,bkhd->bqhd", softmax_weights, value_matrix, preferred_element_type=jnp.float32
    ).astype(jnp.bfloat16)
    out = attended_output.reshape(tokens, feature_width)
    gradient_rows = grad_out.reshape(block_count, BLOCK_TOKENS, head_count, HEAD_SIZE)
    delta = jnp.sum(gradient_rows.astype(jnp.float32) * attended_output.astype(jnp.float32), axis=3)
    delta = jnp.transpose(delta, (0, 2, 1))[..., None]
    probability_gradient = jnp.einsum(
        "bqhd,bkhd->bhqk", gradient_rows, value_matrix, preferred_element_type=jnp.float32
    )
    dscore = (probs * (probability_gradient - delta) * score_scale).astype(jnp.bfloat16)
    query_gradient = jnp.einsum(
        "bhqk,bkhd->bqhd", dscore, key_matrix, preferred_element_type=jnp.float32
    ).astype(jnp.bfloat16)
    query_gradient = query_gradient.reshape(tokens, feature_width)
    key_term = jnp.einsum(
        "bhqk,bqhd->bkhd", dscore, query_matrix, preferred_element_type=jnp.float32
    )
    value_term = jnp.einsum(
        "bhqk,bqhd->bkhd", softmax_weights, gradient_rows, preferred_element_type=jnp.float32
    )
    terms = jnp.concatenate(
        [
            key_term.reshape(block_count, key_count, BLOCK_TOKENS, feature_width),
            value_term.reshape(block_count, key_count, BLOCK_TOKENS, feature_width),
        ],
        axis=3,
    )
    zero_one = jnp.zeros((1, BLOCK_TOKENS, double_width), jnp.float32)
    zero_two = jnp.zeros((2, BLOCK_TOKENS, double_width), jnp.float32)
    ext_grad = (
        jnp.concatenate([terms[:, 0], zero_two], axis=0)
        + jnp.concatenate([zero_one, terms[:, 1], zero_one], axis=0)
        + jnp.concatenate([zero_two, terms[:, 2]], axis=0)
    )
    rims = jnp.concatenate([ext_grad[0], ext_grad[-1]], axis=0)
    returned = extended_2(rims, (("seq", 0),), BLOCK_TOKENS)
    own = ext_grad[1:-1]
    own = own.at[0].add(returned[:BLOCK_TOKENS]).at[-1].add(returned[3 * BLOCK_TOKENS :])
    glob_terms = jnp.sum(terms[:, 3:nfixed], axis=0)
    glob_total = lax.psum(glob_terms, "seq")
    block_ids = jnp.arange(block_count)
    for glob_index in range(nglob):
        owned_here = (block_ids == local_glob[glob_index]) & (owners_glob[glob_index] == myself)
        own = own + jnp.where(owned_here[:, None, None], glob_total[glob_index][None], 0.0)
    tile_terms = terms[:, nfixed:].reshape(needed, BLOCK_TOKENS, double_width).astype(jnp.bfloat16)
    empty = jnp.zeros((nshard * slots,) + tile_terms.shape[1:], tile_terms.dtype)
    arrived = lax.all_to_all(
        empty.at[flat_slot].set(tile_terms).reshape((nshard, slots) + tile_terms.shape[1:]),
        "seq",
        split_axis=0,
        concat_axis=0,
        tiled=True,
    )
    selector = (send_local.reshape(-1)[None, :] == block_ids[:, None]) & valid.reshape(-1)[None, :]
    own = own + jnp.einsum(
        "bs,sqc->bqc",
        selector.astype(jnp.bfloat16),
        arrived.reshape(nshard * slots, BLOCK_TOKENS, double_width),
        preferred_element_type=jnp.float32,
    )
    own = own.reshape(tokens, double_width)
    dkey = own[:, :feature_width].astype(jnp.bfloat16)
    dvalue = own[:, feature_width:].astype(jnp.bfloat16)
    return (out, query_gradient, dkey, dvalue)


def solution(mesh):
    in_specs = (P("seq", "head"), P("seq", "head"), P("seq", "head"), P("seq", "head"), P(), P())
    out_specs = (P("seq", "head"), P("seq", "head"), P("seq", "head"), P("seq", "head"))
    return jax.shard_map(shards, mesh=mesh, in_specs=in_specs, out_specs=out_specs, check_vma=False)
```

profile of v0, /device:TPU:0, one launch (start us, length us, event | category | flops | bytes accessed | tf_op | source)
XLA Modules:
  0.0 201.1 jit_solution(15153234952446303233)
XLA Ops:
  7.2 0.9 constant_dynamic-update-slice_fusion.1
  9.8 0.9 constant_dynamic-update-slice_fusion
  11.4 1.1 broadcast_select_fusion
  12.5 7.4 %all-to-all-start = ((bf16[8,2,64,512]{3,2,1,0:T(8,128)(2,1)}), bf16[8,2,64,512]{3,2,1,0:T(8,128)(2,1)S(1)}, u32[]{:S(2)}, u32[]{:S(2)}) async-start(bf16[8,2,64,512]{3,2,1,0:T(8,128)(2,1)} %broadcast_select_fusion), calls=%async_computation | async-start | bytes 2097152 | tf_op jit(solution)/shard_map/all_to_all | solution.py:67
  19.9 4.8 %collective-permute-start.1 = (bf16[64,512]{1,0:T(8,128)(2,1)S(1)}, bf16[64,512]{1,0:T(8,128)(2,1)S(1)}, u32[]{:S(2)}, u32[]{:S(2)}) collective-permute-start(bf16[64,512]{1,0:T(8,128)(2,1)S(1)} %get-tuple-element.45), channel_id=1, source_target_pairs={{4,0},{8,4},{12,8},{16,12},{20,16},{24,20},{28,24},{0,28},{5,1},{9... | collective-permute-start | bytes 196616 | tf_op jit(solution)/shard_map/ppermute | solution.py:20
  28.3 45.0 %all-reduce.6 = bf16[128,512]{1,0:T(8,128)(2,1)S(1)} all-reduce(f32[128,512]{1,0:T(8,128)S(1)} %pad_maximum_fusion.3), channel_id=1, replica_groups=mesh['seq'=8,'head'=4] {'seq'}, use_global_device_ids=true, to_apply=%region_0.1 | all-reduce | flops 65536 | bytes 393216 | tf_op jit(solution)/shard_map/psum | solution.py:49
  73.5 0.8 constant_dynamic-update-slice_fusion.5
  75.7 0.8 broadcast_dynamic-update-slice_fusion
  77.1 0.9 constant_dynamic-update-slice_fusion.2
  78.0 1.6 fusion.43
  79.6 1.1 reshape.302
  82.7 1.1 multiply_reduce_fusion
  84.3 2.7 %copy.91 = f32[4,448,2,128]{3,2,1,0:T(2,128)} copy(f32[4,448,2,128]{3,1,2,0:T(8,128)S(1)} %convolution_bitcast_fusion) | data formatting | bytes 3670016 | tf_op jit(solution)/shard_map/bhqk,bqhd->bkhd/transpose | solution.py:115
  87.0 2.7 %reshape.309 = f32[4,7,64,256]{3,2,1,0:T(8,128)S(1)} reshape(f32[4,448,2,128]{3,2,1,0:T(2,128)} %copy.91) | data formatting | bytes 3670016 | tf_op jit(solution)/shard_map/reshape | solution.py:121
  90.2 2.7 %copy.89 = f32[4,448,2,128]{3,2,1,0:T(2,128)} copy(f32[4,448,2,128]{3,1,2,0:T(8,128)S(1)} %convolution_bitcast_fusion.1) | data formatting | bytes 3670016 | tf_op jit(solution)/shard_map/bhqk,bqhd->bkhd/transpose | solution.py:112
  92.9 3.6 %reshape.308 = f32[4,7,64,256]{3,2,1,0:T(8,128)} reshape(f32[4,448,2,128]{3,2,1,0:T(2,128)} %copy.89) | data formatting | bytes 3670016 | tf_op jit(solution)/shard_map/reshape | solution.py:120
  96.5 2.0 pad_maximum_fusion
  98.5 1.8 copy-done
  100.6 0.8 scatter_fusion
  101.4 2.1 %copy.99 = bf16[8,2,64,512]{3,1,2,0:T(2,128)(2,1)} copy(bf16[8,2,64,512]{3,2,1,0:T(8,128)(2,1)S(1)} %bitcast.105) | data formatting | bytes 2097152 | tf_op jit(solution)/shard_map/reshape | solution.py:145
  103.4 4.5 %all-to-all-start.1 = ((bf16[8,2,64,512]{3,1,2,0:T(2,128)(2,1)}), bf16[8,2,64,512]{3,1,2,0:T(2,128)(2,1)S(1)}, u32[]{:S(2)}, u32[]{:S(2)}) async-start(bf16[8,2,64,512]{3,1,2,0:T(2,128)(2,1)} %copy.99), calls=%async_computation.1 | async-start | bytes 2097152 | tf_op jit(solution)/shard_map/all_to_all | solution.py:144
  109.5 1.6 fusion.42
  112.5 1.8 collective-permute-start.2
  114.3 2.0 %copy_reduce_fusion = f32[2,64,512]{2,1,0:T(8,128)} fusion(f32[4,7,64,512]{3,2,1,0:T(8,128)} %copy-done), kind=kLoop, calls=%fused_computation.18 | loop fusion | flops 196608 | bytes 1310720 | tf_op jit(solution)/shard_map/reduce_sum | solution.py:136
  116.4 1.4 fusion.6
  117.8 1.2 fusion.12
  120.7 7.4 %collective-permute-done.2 = f32[64,512]{1,0:T(8,128)} collective-permute-done((f32[64,512]{1,0:T(8,128)}, f32[64,512]{1,0:T(8,128)}, u32[]{:S(2)}, u32[]{:S(2)}) %collective-permute-start.2) | collective-permute-done | bytes 131104 | tf_op jit(solution)/shard_map/ppermute | solution.py:17
  128.1 1.0 fusion.21
  129.5 59.6 %all-reduce.5.cloned.1.call-done = f32[2,64,512]{2,1,0:T(8,128)} async-done(((f32[2,64,512]{2,1,0:T(8,128)}), f32[2,64,512]{2,1,0:T(8,128)}) %all-reduce.5.cloned.1.call-update) | async-done | bytes 262160 | tf_op jit(solution)/shard_map/psum | solution.py:137
  189.0 1.0 slice_bitcast_fusion.1
  190.2 1.3 scatter-add.9
  191.5 1.1 copy.100
  (85 shorter events, 15.5 us)
Async XLA Ops:
  11.4 13.3 %copy-start.8 = (s32[2]{0:T(128)S(1)}, s32[2]{0:T(128)}, u32[]{:S(2)}) copy-start(s32[2]{0:T(128)} %param.15) | copy-start | bytes 28
  11.4 15.4 %copy-start.6 = (bf16[256,256]{1,0:T(8,128)(2,1)S(1)}, bf16[256,256]{1,0:T(8,128)(2,1)}, u32[]{:S(2)}) copy-start(bf16[256,256]{1,0:T(8,128)(2,1)} %param.13) | copy-start | bytes 393220
  12.5 15.7 %copy-start.7 = (bf16[256,256]{1,0:T(8,128)(2,1)S(1)}, bf16[256,256]{1,0:T(8,128)(2,1)}, u32[]{:S(2)}) copy-start(bf16[256,256]{1,0:T(8,128)(2,1)} %param.10) | copy-start | bytes 393220
  12.5 64.0 %all-to-all-start = ((bf16[8,2,64,512]{3,2,1,0:T(8,128)(2,1)}), bf16[8,2,64,512]{3,2,1,0:T(8,128)(2,1)S(1)}, u32[]{:S(2)}, u32[]{:S(2)}) async-start(bf16[8,2,64,512]{3,2,1,0:T(8,128)(2,1)} %broadcast_select_fusion), calls=%async_computation | async-start | bytes 2097152 | tf_op jit(solution)/shard_map/all_to_all | solution.py:67
  19.9 53.5 %collective-permute-start.1 = (bf16[64,512]{1,0:T(8,128)(2,1)S(1)}, bf16[64,512]{1,0:T(8,128)(2,1)S(1)}, u32[]{:S(2)}, u32[]{:S(2)}) collective-permute-start(bf16[64,512]{1,0:T(8,128)(2,1)S(1)} %get-tuple-element.45), channel_id=1, source_target_pairs={{4,0},{8,4},{12,8},{16,12},{20,16},{24,20},{28,24},{0,28},{5,1},{9... | collective-permute-start | bytes 196616 | tf_op jit(solution)/shard_map/ppermute | solution.py:20
  24.7 48.7 %collective-permute-start = (bf16[64,512]{1,0:T(8,128)(2,1)S(1)}, bf16[64,512]{1,0:T(8,128)(2,1)S(1)}, u32[]{:S(2)}, u32[]{:S(2)}) collective-permute-start(bf16[64,512]{1,0:T(8,128)(2,1)S(1)} %get-tuple-element.46), channel_id=1, source_target_pairs={{0,4},{4,8},{8,12},{12,16},{16,20},{20,24},{24,28},{28,0},{1,5},{5... | collective-permute-start | bytes 196616 | tf_op jit(solution)/shard_map/ppermute | solution.py:17
  81.5 1.2 copy-start.1
  84.3 5.4 %copy-start.4 = (bf16[4,2,64,448]{3,2,1,0:T(8,128)(2,1)}, bf16[4,2,64,448]{3,2,1,0:T(8,128)(2,1)S(1)}, u32[]{:S(2)}) copy-start(bf16[4,2,64,448]{3,2,1,0:T(8,128)(2,1)S(1)} %fusion.4) | copy-start | bytes 1376260
  98.5 1.8 copy-start
  103.4 88.1 %all-to-all-start.1 = ((bf16[8,2,64,512]{3,1,2,0:T(2,128)(2,1)}), bf16[8,2,64,512]{3,1,2,0:T(2,128)(2,1)S(1)}, u32[]{:S(2)}, u32[]{:S(2)}) async-start(bf16[8,2,64,512]{3,1,2,0:T(2,128)(2,1)} %copy.99), calls=%async_computation.1 | async-start | bytes 2097152 | tf_op jit(solution)/shard_map/all_to_all | solution.py:144
  107.9 81.1 %all-reduce.5.cloned.1.call-start = ((), (), s32[]{:S(2)}) async-start(), calls=%async_computation.2 | async-start | bytes 524288 | tf_op jit(solution)/shard_map/psum | solution.py:137
  111.2 0.7 copy-start.2
  112.5 15.6 %collective-permute-start.2 = (f32[64,512]{1,0:T(8,128)}, f32[64,512]{1,0:T(8,128)}, u32[]{:S(2)}, u32[]{:S(2)}) collective-permute-start(f32[64,512]{1,0:T(8,128)} %fusion.17), channel_id=1, source_target_pairs={{0,4},{4,8},{8,12},{12,16},{16,20},{20,24},{24,28},{28,0},{1,5},{5... | collective-permute-start | bytes 393224 | tf_op jit(solution)/shard_map/ppermute | solution.py:17
  116.4 2.7 %copy-start.5 = (bf16[4,64,2,128]{3,1,2,0:T(8,128)(2,1)S(1)}, bf16[4,64,2,128]{3,1,2,0:T(8,128)(2,1)}, u32[]{:S(2)}) copy-start(bf16[4,64,2,128]{3,1,2,0:T(8,128)(2,1)} %get-tuple-element.56) | copy-start | bytes 393220
  117.8 10.3 %copy-start.3 = (f32[1,64,512]{2,1,0:T(8,128)S(1)}, f32[1,64,512]{2,1,0:T(8,128)}, u32[]{:S(2)}) copy-start(f32[1,64,512]{2,1,0:T(8,128)} %copy-done.2) | copy-start | bytes 393220
  129.4 60.6 %collective-permute-start.3 = (f32[64,512]{1,0:T(8,128)S(1)}, f32[64,512]{1,0:T(8,128)S(1)}, u32[]{:S(2)}, u32[]{:S(2)}) collective-permute-start(f32[64,512]{1,0:T(8,128)S(1)} %get-tuple-element.35), channel_id=1, source_target_pairs={{4,0},{8,4},{12,8},{16,12},{20,16},{24,20},{28,24},{0,28},{5,1},{9... | collective-permute-start | bytes 393224 | tf_op jit(solution)/shard_map/ppermute | solution.py:20
Sparse Core Ops, SparseCore 0:
  116.5 72.4 all-reduce.4
where the time goes:
time: 202 us; the launch traced here: 201 us
  waiting for transfers between devices  67 us (33%)
  blocking collectives  45 us (22%)
  local copies, waits for them, and re-layouts  37.5 us (19%)
  starting transfers between devices  18.8 us (9%)
  between operations  17.1 us (8%)
  other arithmetic  10.5 us (5%)
  matrix products  5.15 us (3%)
    psum x1, waiting for transfers between devices, shards(): glob_total = lax.psum(glob_terms, 'seq')  59.6 us
    psum x1, blocking collectives, shards(): lax.psum(jnp.concatenate(pieces, axis=0), 'seq').astype(jnp.bfloat16)  45 us
    unnamed x30, local copies, waits for them, and re-layouts  8.83 us
    all_to_all x1, starting transfers between devices, shards(): lax.all_to_all(outgoing, 'seq', split_axis=0, concat_axis=0, tiled=True)  7.38 us
    ppermute x2, waiting for transfers between devices, extended_2(): lax.ppermute(lax.slice_in_dim(block, block.shape[dim] - width, None, axis...  7.38 us
    ppermute x2, starting transfers between devices, extended_2(): lax.ppermute(lax.slice_in_dim(block, 0, width, axis=dim), axis, backward)  4.83 us
    all_to_all x1, starting transfers between devices, shards(): lax.all_to_all(empty.at[flat_slot].set(tile_terms).reshape((nshard, slots...  4.53 us
  transfers between devices with their start and end apart: 7, of which 2 were waited for; matrix products, arithmetic and copies ran while one was open for 9% of the time, Pallas kernels for 0%

commit v1 on v0

--- a/solution.py
+++ b/solution.py
@@ -134,7 +134,7 @@
     own = ext_grad[1:-1]
     own = own.at[0].add(returned[:BLOCK_TOKENS]).at[-1].add(returned[3 * BLOCK_TOKENS :])
     glob_terms = jnp.sum(terms[:, 3:nfixed], axis=0)
-    glob_total = lax.psum(glob_terms, "seq")
+    glob_total = jnp.sum(lax.all_gather(glob_terms, "seq"), axis=0)
     block_ids = jnp.arange(block_count)
     for glob_index in range(nglob):
         owned_here = (block_ids == local_glob[glob_index]) & (owners_glob[glob_index] == myself)

time: 202 us -> 174 us (0.86)
  waiting for transfers between devices: 67 us -> 41.2 us
    psum x1 -> x0, waiting for transfers between devices: 59.6 us -> none  [shards(): glob_total = lax.psum(glob_terms, 'seq')]
    ppermute x2, waiting for transfers between devices: 7.38 us -> 22 us  [extended_2(): lax.ppermute(lax.slice_in_dim(block, block.shape[dim] - width, None, axis...]
    all_gather x0 -> x1, waiting for transfers between devices: none -> 14.1 us  [shards(): glob_total = jnp.sum(lax.all_gather(glob_terms, 'seq'), axis=0)]
    ppermute x2, waiting for transfers between devices: 0.01 us -> 5.1 us  [extended_2(): lax.ppermute(lax.slice_in_dim(block, 0, width, axis=dim), axis, backward)]
    unnamed x30 -> x28, local copies, waits for them, and re-layouts: 8.83 us -> 8.94 us
  transfers between devices with their start and end apart: 7 -> 7, of which waited for: 2 -> 3; matrix products, arithmetic and copies ran while one was open for 9% -> 10% of each run, Pallas kernels for 0% -> 0%
where the time goes in v1:
time: 174 us; the launch traced here: 173 us
  blocking collectives  45.3 us (26%)
  waiting for transfers between devices  41.2 us (24%)
  local copies, waits for them, and re-layouts  38 us (22%)
  starting transfers between devices  18.8 us (11%)
  between operations  17.1 us (10%)
  other arithmetic  8.53 us (5%)
  matrix products  4.07 us (2%)
    psum x1, blocking collectives, shards(): lax.psum(jnp.concatenate(pieces, axis=0), 'seq').astype(jnp.bfloat16)  45.3 us
    ppermute x2, waiting for transfers between devices, extended_2(): lax.ppermute(lax.slice_in_dim(block, block.shape[dim] - width, None, axis...  22 us
    all_gather x1, waiting for transfers between devices, shards(): glob_total = jnp.sum(lax.all_gather(glob_terms, 'seq'), axis=0)  14.1 us
    unnamed x28, local copies, waits for them, and re-layouts  8.94 us
    all_to_all x1, starting transfers between devices, shards(): lax.all_to_all(outgoing, 'seq', split_axis=0, concat_axis=0, tiled=True)  7.38 us
    ppermute x2, waiting for transfers between devices, extended_2(): lax.ppermute(lax.slice_in_dim(block, 0, width, axis=dim), axis, backward)  5.1 us
    ppermute x2, starting transfers between devices, extended_2(): lax.ppermute(lax.slice_in_dim(block, 0, width, axis=dim), axis, backward)  4.78 us
    all_to_all x1, starting transfers between devices, shards(): lax.all_to_all(empty.at[flat_slot].set(tile_terms).reshape((nshard, slots...  4.53 us
  transfers between devices with their start and end apart: 7, of which 3 were waited for; matrix products, arithmetic and copies ran while one was open for 10% of the time, Pallas kernels for 0%

profile of v1, /device:TPU:0, one launch (start us, length us, event | category | flops | bytes accessed | tf_op | source)
XLA Modules:
  0.0 173.0 jit_solution(3258275549879798393)
XLA Ops:
  7.2 0.9 constant_dynamic-update-slice_fusion.1
  8.1 0.8 copy.73
  9.8 0.9 constant_dynamic-update-slice_fusion
  11.4 1.1 broadcast_select_fusion
  12.5 7.4 %all-to-all-start = ((bf16[8,2,64,512]{3,2,1,0:T(8,128)(2,1)}), bf16[8,2,64,512]{3,2,1,0:T(8,128)(2,1)S(1)}, u32[]{:S(2)}, u32[]{:S(2)}) async-start(bf16[8,2,64,512]{3,2,1,0:T(8,128)(2,1)} %broadcast_select_fusion), calls=%async_computation | async-start | bytes 2097152 | tf_op jit(solution)/shard_map/all_to_all | solution.py:67
  20.0 4.7 %collective-permute-start.1 = (bf16[64,512]{1,0:T(8,128)(2,1)S(1)}, bf16[64,512]{1,0:T(8,128)(2,1)S(1)}, u32[]{:S(2)}, u32[]{:S(2)}) collective-permute-start(bf16[64,512]{1,0:T(8,128)(2,1)S(1)} %get-tuple-element.45), channel_id=1, source_target_pairs={{4,0},{8,4},{12,8},{16,12},{20,16},{24,20},{28,24},{0,28},{5,1},{9... | collective-permute-start | bytes 196616 | tf_op jit(solution)/shard_map/ppermute | solution.py:20
  28.1 45.3 %all-reduce.3 = bf16[128,512]{1,0:T(8,128)(2,1)S(1)} all-reduce(f32[128,512]{1,0:T(8,128)S(1)} %pad_maximum_fusion.3), channel_id=1, replica_groups=mesh['seq'=8,'head'=4] {'seq'}, use_global_device_ids=true, to_apply=%region_0.1 | all-reduce | flops 65536 | bytes 393216 | tf_op jit(solution)/shard_map/psum | solution.py:49
  75.7 0.8 broadcast_dynamic-update-slice_fusion
  77.1 0.9 constant_dynamic-update-slice_fusion.2
  78.0 1.6 fusion.43
  79.6 1.1 reshape.302
  82.7 1.1 multiply_reduce_fusion
  84.4 2.7 %copy.91 = f32[4,448,2,128]{3,2,1,0:T(2,128)} copy(f32[4,448,2,128]{3,1,2,0:T(8,128)S(1)} %convolution_bitcast_fusion) | data formatting | bytes 3670016 | tf_op jit(solution)/shard_map/bhqk,bqhd->bkhd/transpose | solution.py:115
  87.0 2.7 %reshape.309 = f32[4,7,64,256]{3,2,1,0:T(8,128)S(1)} reshape(f32[4,448,2,128]{3,2,1,0:T(2,128)} %copy.91) | data formatting | bytes 3670016 | tf_op jit(solution)/shard_map/reshape | solution.py:121
  90.2 2.7 %copy.89 = f32[4,448,2,128]{3,2,1,0:T(2,128)} copy(f32[4,448,2,128]{3,1,2,0:T(8,128)S(1)} %convolution_bitcast_fusion.1) | data formatting | bytes 3670016 | tf_op jit(solution)/shard_map/bhqk,bqhd->bkhd/transpose | solution.py:112
  92.9 3.6 %reshape.308 = f32[4,7,64,256]{3,2,1,0:T(8,128)} reshape(f32[4,448,2,128]{3,2,1,0:T(2,128)} %copy.89) | data formatting | bytes 3670016 | tf_op jit(solution)/shard_map/reshape | solution.py:120
  96.5 2.0 %pad_maximum_fusion = f32[4,7,64,512]{3,2,1,0:T(8,128)S(1)} fusion(f32[4,7,64,256]{3,2,1,0:T(8,128)S(1)} %reshape.309, f32[4,7,64,256]{3,2,1,0:T(8,128)} %reshape.308), kind=kLoop, calls=%fused_computation.3 | loop fusion | flops 917504 | bytes 7340032 | tf_op jit(solution)/shard_map/concatenate | solution.py:118
  98.5 1.8 %copy-done = f32[4,7,64,512]{3,2,1,0:T(8,128)} copy-done((f32[4,7,64,512]{3,2,1,0:T(8,128)}, f32[4,7,64,512]{3,2,1,0:T(8,128)S(1)}, u32[]{:S(2)}) %copy-start) | copy-done | bytes 3670040
  100.3 0.8 copy_reduce_fusion
  101.1 1.3 slice.164
  102.6 0.8 scatter_fusion
  103.4 2.1 %copy.99 = bf16[8,2,64,512]{3,1,2,0:T(2,128)(2,1)} copy(bf16[8,2,64,512]{3,2,1,0:T(8,128)(2,1)S(1)} %bitcast.106) | data formatting | bytes 2097152 | tf_op jit(solution)/shard_map/reshape | solution.py:145
  105.5 4.5 %all-to-all-start.1 = ((bf16[8,2,64,512]{3,1,2,0:T(2,128)(2,1)}), bf16[8,2,64,512]{3,1,2,0:T(2,128)(2,1)S(1)}, u32[]{:S(2)}, u32[]{:S(2)}) async-start(bf16[8,2,64,512]{3,1,2,0:T(2,128)(2,1)} %copy.99), calls=%async_computation.1 | async-start | bytes 2097152 | tf_op jit(solution)/shard_map/all_to_all | solution.py:144
  111.6 1.6 fusion.42
  113.3 2.1 %collective-permute-start.2 = (f32[64,512]{1,0:T(8,128)S(1)}, f32[64,512]{1,0:T(8,128)S(1)}, u32[]{:S(2)}, u32[]{:S(2)}) collective-permute-start(f32[64,512]{1,0:T(8,128)S(1)} %fusion.17), channel_id=1, source_target_pairs={{0,4},{4,8},{8,12},{12,16},{16,20},{20,24},{24,28},{28,0},{1,5},{5... | collective-permute-start | bytes 393224 | tf_op jit(solution)/shard_map/ppermute | solution.py:17
  115.6 22.0 %collective-permute-done.2 = f32[64,512]{1,0:T(8,128)S(1)} collective-permute-done((f32[64,512]{1,0:T(8,128)S(1)}, f32[64,512]{1,0:T(8,128)S(1)}, u32[]{:S(2)}, u32[]{:S(2)}) %collective-permute-start.2) | collective-permute-done | bytes 131104 | tf_op jit(solution)/shard_map/ppermute | solution.py:17
  140.1 5.1 %collective-permute-done.3 = f32[64,512]{1,0:T(8,128)S(1)} collective-permute-done((f32[64,512]{1,0:T(8,128)S(1)}, f32[64,512]{1,0:T(8,128)S(1)}, u32[]{:S(2)}, u32[]{:S(2)}) %collective-permute-start.3) | collective-permute-done | bytes 131104 | tf_op jit(solution)/shard_map/ppermute | solution.py:20
  145.4 1.3 scatter-add.9
  146.7 0.8 copy-done.3
  147.4 1.1 copy.100
  149.1 14.1 %all-gather.3.cloned.1.call-done = f32[16,64,512]{2,1,0:T(8,128)} async-done(((f32[2,64,512]{2,1,0:T(8,128)}), f32[16,64,512]{2,1,0:T(8,128)}) %all-gather.3.cloned.1.call-update) | async-done | bytes 2097168 | tf_op jit(solution)/shard_map/all_gather | solution.py:137
  163.1 1.8 %reduce_sum.62 = f32[2,64,512]{2,1,0:T(8,128)S(1)} reduce(f32[8,2,64,512]{3,2,1,0:T(8,128)} %bitcast.109, f32[]{:T(128)} %constant.128.clone.1), dimensions={0}, to_apply=%region_8.9 | reduce | flops 458752 | bytes 2359300 | tf_op jit(solution)/shard_map/reduce_sum | solution.py:137
  (84 shorter events, 14.5 us)
Async XLA Ops:
  11.4 13.3 %copy-start.7 = (s32[2]{0:T(128)S(1)}, s32[2]{0:T(128)}, u32[]{:S(2)}) copy-start(s32[2]{0:T(128)} %param.15) | copy-start | bytes 28
  11.4 15.2 %copy-start.5 = (bf16[256,256]{1,0:T(8,128)(2,1)S(1)}, bf16[256,256]{1,0:T(8,128)(2,1)}, u32[]{:S(2)}) copy-start(bf16[256,256]{1,0:T(8,128)(2,1)} %param.13) | copy-start | bytes 393220
  12.5 15.5 %copy-start.6 = (bf16[256,256]{1,0:T(8,128)(2,1)S(1)}, bf16[256,256]{1,0:T(8,128)(2,1)}, u32[]{:S(2)}) copy-start(bf16[256,256]{1,0:T(8,128)(2,1)} %param.10) | copy-start | bytes 393220
  12.5 64.0 %all-to-all-start = ((bf16[8,2,64,512]{3,2,1,0:T(8,128)(2,1)}), bf16[8,2,64,512]{3,2,1,0:T(8,128)(2,1)S(1)}, u32[]{:S(2)}, u32[]{:S(2)}) async-start(bf16[8,2,64,512]{3,2,1,0:T(8,128)(2,1)} %broadcast_select_fusion), calls=%async_computation | async-start | bytes 2097152 | tf_op jit(solution)/shard_map/all_to_all | solution.py:67
  19.9 143.2 %all-gather.3.cloned.1.call-start = ((), (), s32[]{:S(2)}) async-start(), calls=%async_computation.2 | async-start | bytes 2359296 | tf_op jit(solution)/shard_map/all_gather | solution.py:137
  20.0 53.4 %collective-permute-start.1 = (bf16[64,512]{1,0:T(8,128)(2,1)S(1)}, bf16[64,512]{1,0:T(8,128)(2,1)S(1)}, u32[]{:S(2)}, u32[]{:S(2)}) collective-permute-start(bf16[64,512]{1,0:T(8,128)(2,1)S(1)} %get-tuple-element.45), channel_id=1, source_target_pairs={{4,0},{8,4},{12,8},{16,12},{20,16},{24,20},{28,24},{0,28},{5,1},{9... | collective-permute-start | bytes 196616 | tf_op jit(solution)/shard_map/ppermute | solution.py:20
  24.7 48.7 %collective-permute-start = (bf16[64,512]{1,0:T(8,128)(2,1)S(1)}, bf16[64,512]{1,0:T(8,128)(2,1)S(1)}, u32[]{:S(2)}, u32[]{:S(2)}) collective-permute-start(bf16[64,512]{1,0:T(8,128)(2,1)S(1)} %get-tuple-element.46), channel_id=1, source_target_pairs={{0,4},{4,8},{8,12},{12,16},{16,20},{20,24},{24,28},{28,0},{1,5},{5... | collective-permute-start | bytes 196616 | tf_op jit(solution)/shard_map/ppermute | solution.py:17
  81.5 1.2 copy-start.1
  98.5 1.8 %copy-start = (f32[4,7,64,512]{3,2,1,0:T(8,128)}, f32[4,7,64,512]{3,2,1,0:T(8,128)S(1)}, u32[]{:S(2)}) copy-start(f32[4,7,64,512]{3,2,1,0:T(8,128)S(1)} %pad_maximum_fusion) | copy-start | bytes 11010052
  105.5 42.0 %all-to-all-start.1 = ((bf16[8,2,64,512]{3,1,2,0:T(2,128)(2,1)}), bf16[8,2,64,512]{3,1,2,0:T(2,128)(2,1)S(1)}, u32[]{:S(2)}, u32[]{:S(2)}) async-start(bf16[8,2,64,512]{3,1,2,0:T(2,128)(2,1)} %copy.99), calls=%async_computation.1 | async-start | bytes 2097152 | tf_op jit(solution)/shard_map/all_to_all | solution.py:144
  113.3 24.3 %collective-permute-start.2 = (f32[64,512]{1,0:T(8,128)S(1)}, f32[64,512]{1,0:T(8,128)S(1)}, u32[]{:S(2)}, u32[]{:S(2)}) collective-permute-start(f32[64,512]{1,0:T(8,128)S(1)} %fusion.17), channel_id=1, source_target_pairs={{0,4},{4,8},{8,12},{12,16},{16,20},{20,24},{24,28},{28,0},{1,5},{5... | collective-permute-start | bytes 393224 | tf_op jit(solution)/shard_map/ppermute | solution.py:17
  115.6 22.5 %copy-start.2 = (bf16[4,64,2,128]{3,1,2,0:T(8,128)(2,1)S(1)}, bf16[4,64,2,128]{3,1,2,0:T(8,128)(2,1)}, u32[]{:S(2)}) copy-start(bf16[4,64,2,128]{3,1,2,0:T(8,128)(2,1)} %get-tuple-element.56) | copy-start | bytes 393220
  137.7 7.5 %collective-permute-start.3 = (f32[64,512]{1,0:T(8,128)S(1)}, f32[64,512]{1,0:T(8,128)S(1)}, u32[]{:S(2)}, u32[]{:S(2)}) collective-permute-start(f32[64,512]{1,0:T(8,128)S(1)} %get-tuple-element.35), channel_id=1, source_target_pairs={{4,0},{8,4},{12,8},{16,12},{20,16},{24,20},{28,24},{0,28},{5,1},{9... | collective-permute-start | bytes 393224 | tf_op jit(solution)/shard_map/ppermute | solution.py:20
  146.7 0.8 copy-start.3
  149.0 15.9 %copy-start.4 = (f32[4,64,512]{2,0,1:T(4,128)S(1)}, f32[4,64,512]{2,0,1:T(4,128)}, u32[]{:S(2)}) copy-start(f32[4,64,512]{2,0,1:T(4,128)} %copy-done.3) | copy-start | bytes 1572868
Sparse Core Ops, SparseCore 0:
  101.3 61.8 all-gather.2
